TPU v7x, 32 devices: a whole 2x2x4 slice. The times are simulated.
32 devices in a mesh: seq: 8 (over z, y), head: 4 (over x, core).
Axes of the slice: x: 2, y: 2, z: 4, core: 2. Of those that a mesh axis runs over, the one named last changes fastest.
Arguments:
- queries: bfloat16 [4096, 6144], P('seq', 'head'), may hold values from -6 to 6
- keys: bfloat16 [4096, 6144], P('seq', 'head'), may hold values from -6 to 6
- values: bfloat16 [4096, 6144], P('seq', 'head'), may hold values from -6 to 6
- attn_out: bfloat16 [4096, 6144], P('seq', 'head'), may hold values from -120 to 120
- out_grad: bfloat16 [4096, 6144], P('seq', 'head'), may hold values from -6 to 6
- norm_gain: float32 [6144], P('head'), may hold values from 0.5 to 2
Outputs:
- query_grad: bfloat16 [4096, 6144], P('seq', 'head')
- key_grad: bfloat16 [4096, 6144], P('seq', 'head')
- value_grad: bfloat16 [4096, 6144], P('seq', 'head')
All inputs are finite; a program needn't handle non-finite values.
Results may differ from a plain program's by a relative error of at most 0.0057.
Values sent between devices are 32-bit elements; how exact they have to be, the bound alone decides.
A program may use at most 128 MiB of HBM per device.

v0:
```python
import functools
import math

import jax
import jax.numpy as jnp
from jax import lax
from jax.experimental import pallas as pl
from jax.experimental.pallas import tpu as pltpu
from jax.sharding import PartitionSpec as P

DH = 128
GROUP = 256
EPS = 1e-06
MESH = pl.DeviceIdType.MESH
F32 = jnp.float32
BF16 = jnp.bfloat16
LAG = 6
EARLY = 5
HOP = 3
SETTLE = 3
STORES = 4


def dot(a, b, ca, cb):
    return lax.dot_general(a, b, (((ca,), (cb,)), ((), ())), preferred_element_type=F32)


def split_seq(count):
    inner = 1
    while inner * inner * 4 <= count:
        inner *= 2
    while count % inner:
        inner //= 2
    return count // inner, inner


def kernel(
    cfg,
    q_hbm, k_hbm, v_hbm, o_hbm, d_hbm, gain_hbm,
    qg_out, kg_out, vg_out,
    q_ref, k_ref, v_ref, o_ref, d_ref, gain_ref,
    acc_q, acc_k, acc_v, terms, slots, zin, inc, sums,
    load_sem, sum_send, sum_recv, y_send, y_recv, z_send, z_recv,
):
    zs, ys, hs, heads, ch, raw, rows, full_width, factor = cfg
    n = heads // ch
    blocks = rows // GROUP
    seq = lax.axis_index("seq")
    mine = lax.axis_index("head")
    z = seq // ys
    y = seq % ys
    hops = (z, zs - 1 - z)
    steps = (zs - 1) * HOP + LAG + n

    loads = [
        pltpu.make_async_copy(src, dst, load_sem.at[i])
        for i, (src, dst) in enumerate(
            ((k_hbm, k_ref), (v_hbm, v_ref), (o_hbm, o_ref), (d_hbm, d_ref), (q_hbm, q_ref))
        )
    ]
    for load in loads:
        load.start()
    gain_load = pltpu.make_async_copy(gain_hbm, gain_ref, load_sem.at[5])
    gain_load.start()

    barrier = pltpu.get_barrier_semaphore()

    def greet(s, h):
        pl.semaphore_signal(barrier, inc=1, device_id=(s, h), device_id_type=MESH)

    for d in range(1, hs):
        greet(seq, lax.rem(mine + d, hs))
    for d in range(1, ys):
        greet(z * ys + lax.rem(y + d, ys), mine)

    @pl.when(z > 0)
    def _():
        greet(seq - ys, mine)

    @pl.when(z < zs - 1)
    def _():
        greet(seq + ys, mine)

    for kind in range(2):

        @pl.when(hops[kind] == 0)
        def _():
            zin[kind] = jnp.zeros_like(zin[kind])

    def chunk(c):
        return pl.ds(c * ch, ch)

    def lanes(h):
        return pl.ds(pl.multiple_of(h * DH, DH), DH)

    def toks(b):
        return slice(b * GROUP, (b + 1) * GROUP)

    def y_copy(kind, src, c, d):
        other = lax.rem(y + d, ys)
        return pltpu.make_async_remote_copy(
            src_ref=src.at[chunk(c)],
            dst_ref=slots.at[kind, y, chunk(c)],
            send_sem=y_send.at[kind, d - 1, c],
            recv_sem=y_recv.at[kind, y, c],
            device_id=(z * ys + other, mine),
            device_id_type=MESH,
        )

    def y_arrive(kind, c, d):
        other = lax.rem(y + d, ys)
        pltpu.make_async_remote_copy(
            src_ref=slots.at[kind, other, chunk(c)],
            dst_ref=slots.at[kind, other, chunk(c)],
            send_sem=y_send.at[kind, d - 1, c],
            recv_sem=y_recv.at[kind, other, c],
            device_id=(z * ys + other, mine),
            device_id_type=MESH,
        ).wait_recv()

    def z_copy(kind, c):
        return pltpu.make_async_remote_copy(
            src_ref=inc.at[kind, chunk(c)],
            dst_ref=zin.at[kind, chunk(c)],
            send_sem=z_send.at[kind, c],
            recv_sem=z_recv.at[kind, c],
            device_id=(seq + (ys if kind == 0 else -ys), mine),
            device_id_type=MESH,
        )

    def later(kind, other):
        return other > y if kind == 0 else other < y

    def raw_sent(kind, d):
        return later(kind, lax.rem(y + d, ys)) | (hops[kind] < zs - 1)

    def own_terms(kind, a_ref, b_ref):
        def one(c, carry):
            for i in range(ch):
                h = c * ch + i
                total = None
                for b in range(blocks):
                    part = dot(a_ref[toks(b), lanes(h)], b_ref[toks(b), lanes(h)], 0, 0)
                    terms[kind, b, h] = part
                    total = part if total is None else total + part
                slots[kind, y, h] = total

            @pl.when(c < raw)
            def _():
                for d in range(1, ys):

                    @pl.when(raw_sent(kind, d))
                    def _():
                        y_copy(kind, slots.at[kind, y], c, d).start()

            @pl.when((c >= raw) & (hops[kind] == 0))
            def _():
                step(kind, c - raw, 0)

            return carry

        lax.fori_loop(0, n, one, 0)

    def step(kind, place, first):
        @pl.when((place >= first) & (place < n))
        def _():
            c = lax.rem(place + raw, n)

            @pl.when(hops[kind] > 0)
            def _():
                z_copy(kind, c).wait_recv()

            @pl.when(place >= n - raw)
            def _():
                for d in range(1, ys):
                    other = lax.rem(y + d, ys)

                    @pl.when(jnp.logical_not(later(kind, other)) | (hops[kind] < zs - 1))
                    def _():
                        y_arrive(kind, c, d)

                @pl.when(hops[kind] < zs - 1)
                def _():
                    total = zin[kind, chunk(c)]
                    for s in range(ys):
                        total = total + slots[kind, s, chunk(c)]
                    inc[kind, chunk(c)] = total

            @pl.when(place < n - raw)
            def _():
                inc[kind, chunk(c)] = zin[kind, chunk(c)] + slots[kind, y, chunk(c)]
                for d in range(1, ys):
                    other = lax.rem(y + d, ys)

                    @pl.when(later(kind, other))
                    def _():
                        y_copy(kind, inc.at[kind], c, d).start()

                    @pl.when(jnp.logical_not(later(kind, other)) & (hops[kind] > 0))
                    def _():
                        y_copy(kind, zin.at[kind], c, d).start()

            @pl.when(hops[kind] < zs - 1)
            def _():
                z_copy(kind, c).start()

    def start(kind):
        return jnp.where(hops[kind] == 0, EARLY - n + raw, hops[kind] * HOP + kind * LAG)

    loads[0].wait()
    loads[1].wait()
    peers = hs - 1 + ys - 1 + jnp.where(z > 0, 1, 0) + jnp.where(z < zs - 1, 1, 0)
    pl.semaphore_wait(barrier, peers)
    own_terms(0, k_ref, v_ref)

    loads[2].wait()
    loads[3].wait()
    gain_load.wait()
    tile = 128
    for r in range(rows // tile):
        rs = slice(r * tile, (r + 1) * tile)

        def partial(h, carry):
            sq, cr = carry
            of = o_ref[rs, lanes(h)].astype(F32)
            sc = gain_ref[lanes(h)][None, :] * d_ref[rs, lanes(h)].astype(F32)
            return sq + of * of, cr + sc * of

        zero = jnp.zeros((tile, DH), F32)
        sq, cr = lax.fori_loop(0, heads, partial, (zero, zero))
        sq = jnp.sum(sq.T, axis=0, keepdims=True)
        cr = jnp.sum(cr.T, axis=0, keepdims=True)
        sums[mine, 0:4, rs] = jnp.broadcast_to(sq, (4, tile))
        sums[mine, 4:8, rs] = jnp.broadcast_to(cr, (4, tile))

    def sum_copy(slot, d):
        return pltpu.make_async_remote_copy(
            src_ref=sums.at[slot],
            dst_ref=sums.at[slot],
            send_sem=sum_send.at[d - 1],
            recv_sem=sum_recv.at[slot],
            device_id=(seq, lax.rem(mine + d, hs)),
            device_id_type=MESH,
        )

    for d in range(1, hs):
        sum_copy(mine, d).start()
    for t in range(EARLY):
        step(0, t - start(0), jnp.where(z == 0, n - raw, 0))
    for d in range(1, hs):
        sum_copy(lax.rem(mine + d, hs), d).wait_recv()
    total = sums[0]
    for s in range(1, hs):
        total = total + sums[s]
    rms = jnp.sqrt(total[0:1] / full_width + EPS)
    inv_row = 1.0 / rms
    coef_row = total[4:5] / (full_width * (rms * rms * rms))
    for r in range(rows // tile):
        rs = slice(r * tile, (r + 1) * tile)
        inv = jnp.broadcast_to(inv_row[:, rs], (tile, tile)).T
        coef = jnp.broadcast_to(coef_row[:, rs], (tile, tile)).T

        def normed(h, carry):
            of = o_ref[rs, lanes(h)].astype(F32)
            sc = gain_ref[lanes(h)][None, :] * d_ref[rs, lanes(h)].astype(F32)
            d_ref[rs, lanes(h)] = (sc * inv - of * coef).astype(BF16)
            return carry

        lax.fori_loop(0, heads, normed, 0)

    loads[4].wait()
    own_terms(1, q_ref, d_ref)

    def local(c):
        row = lax.broadcasted_iota(jnp.int32, (GROUP, GROUP), 0)
        col = lax.broadcasted_iota(jnp.int32, (GROUP, GROUP), 1)
        for i in range(ch):
            h = c * ch + i
            for b in range(blocks):
                qb = q_ref[toks(b), lanes(h)]
                kb = k_ref[toks(b), lanes(h)]
                vb = v_ref[toks(b), lanes(h)]
                gb = d_ref[toks(b), lanes(h)]
                prods = jnp.where(row >= col, dot(gb, vb, 1, 1), 0.0).astype(BF16)
                acc_q[toks(b), lanes(h)] = dot(prods, kb, 1, 0)
                prods_t = jnp.where(col >= row, dot(vb, gb, 1, 1), 0.0).astype(BF16)
                acc_k[toks(b), lanes(h)] = dot(prods_t, qb, 1, 0)
                scores_t = jnp.where(col >= row, dot(kb, qb, 1, 1), 0.0).astype(BF16)
                acc_v[toks(b), lanes(h)] = dot(scores_t, gb, 1, 0)

    def finish(c):
        @pl.when(c >= raw)
        def _():
            for kind in range(2):
                for d in range(1, ys):
                    other = lax.rem(y + d, ys)

                    @pl.when(jnp.logical_not(later(kind, other)) | (hops[kind] > 0))
                    def _():
                        y_arrive(kind, c, d)

        for i in range(ch):
            h = c * ch + i
            ends = []
            for kind in range(2):
                total = zin[kind, h]
                for d in range(1, ys):
                    other = lax.rem(y + d, ys)
                    used = jnp.logical_not(later(kind, other)) | ((c >= raw) & (hops[kind] > 0))
                    total = total + jnp.where(used, slots[kind, other, h], 0.0)
                ends.append(total)
            fwd, bwd = [ends[0]], [ends[1]]
            for b in range(blocks - 1):
                fwd.append(fwd[-1] + terms[0, b, h])
                bwd.insert(0, bwd[0] + terms[1, blocks - 1 - b, h])
            for b in range(blocks):
                at = (toks(b), lanes(h))
                kb, vb, gb = k_ref[at], v_ref[at], d_ref[at]
                fs, bs = fwd[b].astype(BF16), bwd[b].astype(BF16)
                qg_out[at] = ((acc_q[at] + dot(gb, fs, 1, 1)) * factor).astype(BF16)
                kg_out[at] = ((acc_k[at] + dot(vb, bs, 1, 1)) * factor).astype(BF16)
                vg_out[at] = ((acc_v[at] + dot(kb, bs, 1, 0)) * factor).astype(BF16)

    last = jnp.maximum(start(0), start(1))
    edge = (hops[0] == 0) | (hops[1] == 0)

    def turn(t, carry):
        for kind in range(2):
            step(kind, t - start(kind), jnp.where(hops[kind] == 0, n - raw, 0))

        @pl.when(t - EARLY < n)
        def _():
            local(t - EARLY)

        place = t - last

        @pl.when((place >= n - raw) & (place < n))
        def _():
            finish(lax.rem(place + raw, n))

        settled = place - SETTLE

        @pl.when(edge & (settled >= 0) & (settled < n - raw))
        def _():
            finish(settled + raw)

        return carry

    lax.fori_loop(EARLY, steps + SETTLE, turn, 0)

    @pl.when(jnp.logical_not(edge))
    def _():
        lax.fori_loop(raw, n, lambda c, carry: (finish(c), carry)[1], 0)

    for d in range(1, hs):
        sum_copy(mine, d).wait_send()

    def sent(c, carry):
        for kind in range(2):
            for d in range(1, ys):
                other = lax.rem(y + d, ys)

                begun = jnp.where(c < raw, hops[kind] < zs - 1, hops[kind] > 0)

                @pl.when(later(kind, other) | begun)
                def _():
                    y_copy(kind, inc.at[kind], c, d).wait_send()

            @pl.when(hops[kind] < zs - 1)
            def _():
                z_copy(kind, c).wait_send()

        return carry

    lax.fori_loop(0, n, sent, 0)


def store_kernel(a, b, c, a_out, b_out, c_out, sem):
    part = a.shape[0] // STORES
    copies = []
    for i in range(STORES):
        at = slice(i * part, (i + 1) * part)
        for j, (src, dst) in enumerate(((a, a_out), (b, b_out), (c, c_out))):
            copies.append(pltpu.make_async_copy(src.at[at], dst.at[at], sem.at[j, i]))
    for copy in copies:
        copy.start()
    for copy in copies:
        copy.wait()


def shards(sizes, queries, keys, values, attn_out, out_grad, norm_gain):
    seqs, hs = sizes
    zs, ys = split_seq(seqs)
    rows, width = queries.shape
    heads = width // DH
    blocks = rows // GROUP
    ch = 1
    n = heads // ch
    raw = n // 2
    factor = 1.0 / math.sqrt(DH * rows * seqs)
    cfg = (zs, ys, hs, heads, ch, raw, rows, width * hs, factor)
    big = pltpu.VMEM((rows, width), BF16)
    acc = pltpu.VMEM((rows, width), F32)
    state = (heads, DH, DH)
    out = jax.ShapeDtypeStruct((rows, width), BF16)
    dma = pltpu.SemaphoreType.DMA
    flops = 2 * heads * blocks * (6 * GROUP * GROUP * DH + 5 * GROUP * DH * DH)
    held = pl.pallas_call(
        functools.partial(kernel, cfg),
        out_shape=(out, out, out),
        in_specs=[pl.BlockSpec(memory_space=pltpu.HBM)] * 6,
        out_specs=[pl.BlockSpec(memory_space=pltpu.VMEM)] * 3,
        scratch_shapes=[
            big, big, big, big, big,
            pltpu.VMEM((width,), F32),
            acc, acc, acc,
            pltpu.VMEM((2, blocks) + state, F32),
            pltpu.VMEM((2, ys) + state, F32),
            pltpu.VMEM((2,) + state, F32),
            pltpu.VMEM((2,) + state, F32),
            pltpu.VMEM((hs, 8, rows), F32),
            dma((6,)),
            dma((hs - 1,)),
            dma((hs,)),
            dma((2, ys - 1, n)),
            dma((2, ys, n)),
            dma((2, n)),
            dma((2, n)),
        ],
        cost_estimate=pl.CostEstimate(
            flops=flops, bytes_accessed=8 * rows * width * 2, transcendentals=0
        ),
        compiler_params=pltpu.CompilerParams(
            collective_id=0, has_side_effects=True, vmem_limit_bytes=42 * 1024 * 1024
        ),
    )(*[
        pltpu.with_memory_space_constraint(x, pltpu.HBM)
        for x in (queries, keys, values, attn_out, out_grad, norm_gain)
    ])
    return pl.pallas_call(
        store_kernel,
        out_shape=(out, out, out),
        in_specs=[pl.BlockSpec(memory_space=pl.ANY)] * 3,
        out_specs=[pl.BlockSpec(memory_space=pltpu.HBM)] * 3,
        scratch_shapes=[dma((3, STORES))],
        cost_estimate=pl.CostEstimate(
            flops=0, bytes_accessed=3 * rows * width * 2, transcendentals=0
        ),
        compiler_params=pltpu.CompilerParams(vmem_limit_bytes=4 * 1024 * 1024),
    )(*held)


def solution(mesh):
    sizes = (mesh.shape["seq"], mesh.shape["head"])
    spec = P("seq", "head")
    return jax.shard_map(
        functools.partial(shards, sizes),
        mesh=mesh,
        in_specs=(spec,) * 5 + (P("head"),),
        out_specs=(spec,) * 3,
        check_vma=False,
    )
```

profile of v0, /device:TPU:0, one launch (start us, length us, event | category | flops | bytes accessed | tf_op | source)
XLA Modules:
  0.0 48.3 jit_solution(8733474436302651415)
XLA Ops:
  0.6 45.4 %shard_map.85 = (bf16[512,1536]{1,0:T(8,128)(2,1)S(1)}, bf16[512,1536]{1,0:T(8,128)(2,1)S(1)}, bf16[512,1536]{1,0:T(8,128)(2,1)S(1)}) custom-call(bf16[512,1536]{1,0:T(8,128)(2,1)} %q_hbm.1, bf16[512,1536]{1,0:T(8,128)(2,1)} %k_hbm.1, bf16[512,1536]{1,0:T(8,128)(2,1)} %v_hbm.1, bf16[512,1536]{1,0:T(8,128)(2,1)} %o_hbm.1, bf16[512,1536]{1,0:T(8,128)(2,1)} %d_hbm.1, ...), custom_call_target="tpu_custom_call" | custom-call | flops 3422552064 | bytes 12582912 | tf_op jit(solution)/shard_map/pallas_call | solution.py:408
  46.0 2.3 %shard_map.86 = (bf16[512,1536]{1,0:T(8,128)(2,1)}, bf16[512,1536]{1,0:T(8,128)(2,1)}, bf16[512,1536]{1,0:T(8,128)(2,1)}) custom-call(bf16[512,1536]{1,0:T(8,128)(2,1)S(1)} %get-tuple-element.6.a, bf16[512,1536]{1,0:T(8,128)(2,1)S(1)} %get-tuple-element.7.b, bf16[512,1536]{1,0:T(8,128)(2,1)S(1)} %get-tuple-element.8.c), custom_call_target="tpu_custom_call" | custom-call | bytes 4718592 | tf_op jit(solution)/shard_map/pallas_call | solution.py:440
where the time goes:
time: 48.5 us; the launch traced here: 48.3 us
  Pallas kernels  47.7 us (98%)
  between operations  0.64 us (1%)
    pallas_call x1, Pallas kernels, shards(): pl.pallas_call(functools.partial(kernel, cfg), out_shape=(out, out, out),...  45.4 us
    pallas_call x1, Pallas kernels, shards(): pl.pallas_call(store_kernel, out_shape=(out, out, out), in_specs=[pl.Bloc...  2.27 us

commit v1 on v0

--- a/solution.py
+++ b/solution.py
@@ -396,7 +396,7 @@
     blocks = rows // GROUP
     ch = 1
     n = heads // ch
-    raw = n // 2
+    raw = n // 3
     factor = 1.0 / math.sqrt(DH * rows * seqs)
     cfg = (zs, ys, hs, heads, ch, raw, rows, width * hs, factor)
     big = pltpu.VMEM((rows, width), BF16)

time: 48.5 us -> 48.5 us (level)
  no operation moved by 1% of the time
where the time goes in v1:
time: 48.5 us; the launch traced here: 48.3 us
  Pallas kernels  47.7 us (98%)
  between operations  0.64 us (1%)
    pallas_call x1, Pallas kernels, shards(): pl.pallas_call(functools.partial(kernel, cfg), out_shape=(out, out, out),...  45.4 us
    pallas_call x1, Pallas kernels, shards(): pl.pallas_call(store_kernel, out_shape=(out, out, out), in_specs=[pl.Bloc...  2.27 us

profile of v1, /device:TPU:0, one launch (start us, length us, event | category | flops | bytes accessed | tf_op | source)
XLA Modules:
  0.0 48.3 jit_solution(10164482071753285905)
XLA Ops:
  0.6 45.4 %shard_map.85 = (bf16[512,1536]{1,0:T(8,128)(2,1)S(1)}, bf16[512,1536]{1,0:T(8,128)(2,1)S(1)}, bf16[512,1536]{1,0:T(8,128)(2,1)S(1)}) custom-call(bf16[512,1536]{1,0:T(8,128)(2,1)} %q_hbm.1, bf16[512,1536]{1,0:T(8,128)(2,1)} %k_hbm.1, bf16[512,1536]{1,0:T(8,128)(2,1)} %v_hbm.1, bf16[512,1536]{1,0:T(8,128)(2,1)} %o_hbm.1, bf16[512,1536]{1,0:T(8,128)(2,1)} %d_hbm.1, ...), custom_call_target="tpu_custom_call" | custom-call | flops 3422552064 | bytes 12582912 | tf_op jit(solution)/shard_map/pallas_call | solution.py:408
  46.0 2.3 %shard_map.86 = (bf16[512,1536]{1,0:T(8,128)(2,1)}, bf16[512,1536]{1,0:T(8,128)(2,1)}, bf16[512,1536]{1,0:T(8,128)(2,1)}) custom-call(bf16[512,1536]{1,0:T(8,128)(2,1)S(1)} %get-tuple-element.6.a, bf16[512,1536]{1,0:T(8,128)(2,1)S(1)} %get-tuple-element.7.b, bf16[512,1536]{1,0:T(8,128)(2,1)S(1)} %get-tuple-element.8.c), custom_call_target="tpu_custom_call" | custom-call | bytes 4718592 | tf_op jit(solution)/shard_map/pallas_call | solution.py:440
